TPU v7x, 32 devices: a whole 2x2x4 slice. The times are simulated.
32 devices in a mesh: row: 8 (over y, x, core), col: 4 (over z).
Axes of the slice: x: 2, y: 2, z: 4, core: 2. Of those that a mesh axis runs over, the one named last changes fastest.
Arguments:
- traces: bfloat16 [2048, 64, 512], P(('row', 'col')), may hold values from -6 to 6
- live_flags: int32 [2048], P(('row', 'col')), may hold values 0 or 1
Outputs:
- correlations: bfloat16 [2048, 2048, 128], P('row', 'col')
Inputs may be any that keep to these rules, and one draw needn't show every extreme that they name: `live_flags`: 1 marks a working channel.
All inputs are finite; a program needn't handle non-finite values. No bound on the sum of `live_flags` on one device may be relied on, other than what follows from the above.
Results may differ from a plain program's by a relative error of at most 0.0058.
Values may be sent and summed in bfloat16 or wider, within the bound.
A program may use at most 448 MiB of HBM per device.

v0:
```python
import math

import jax
import jax.numpy as jnp
from jax import lax
from jax.sharding import PartitionSpec as P

F = 256
LAGS = 128
SAMP = 512
NW = 64


def make_tables():
    samples = jnp.arange(SAMP, dtype=jnp.int32)
    bins = jnp.arange(F, dtype=jnp.int32)
    phase = samples[:, None] * bins[None, :] % SAMP
    angle = 2.0 * math.pi * phase.astype(jnp.float32) / SAMP
    forward = jnp.concatenate([jnp.cos(angle), -jnp.sin(angle)], axis=1)
    taper = 0.5 - 0.5 * jnp.cos(2.0 * math.pi * samples.astype(jnp.float32) / SAMP)
    near = (jnp.abs(bins[:, None] - bins[None, :]) <= 4).astype(jnp.float32)
    counts = jnp.sum(near, axis=0)
    lagval = jnp.arange(LAGS, dtype=jnp.int32) - LAGS // 2
    lphase = bins[:, None] * lagval[None, :] % SAMP
    langle = 2.0 * math.pi * lphase.astype(jnp.float32) / SAMP
    inverse = jnp.concatenate([jnp.cos(langle), -jnp.sin(langle)], axis=0).astype(jnp.bfloat16)
    return (forward, taper, near, counts, inverse)


def whiten(traces, live_flags, forward, taper, near, counts):
    chans = traces.shape[0]
    tapered = traces.astype(jnp.float32) * taper
    spectra = jnp.dot(tapered.reshape(-1, SAMP), forward, precision=lax.Precision.HIGHEST)
    real_part = spectra[:, :F]
    imag_part = spectra[:, F:]
    power = real_part * real_part + imag_part * imag_part
    smooth = jnp.dot(power, near, precision=lax.Precision.HIGHEST) / counts
    level = jnp.mean(power, axis=1, keepdims=True)
    scale = 1.0 / jnp.sqrt(smooth + 0.05 * level + 1e-06)
    alive = jnp.repeat(live_flags.astype(jnp.float32), NW)[:, None]
    white = jnp.concatenate([real_part * scale, imag_part * scale], axis=1) * alive
    white = white.reshape(chans, NW, 2, F)
    white = jnp.transpose(white, (3, 0, 2, 1)).reshape(F, chans, 2 * NW)
    return white.astype(jnp.bfloat16)


def cross_terms(first, second):
    half = first.shape[-1] // 2
    turned = jnp.concatenate([first[..., half:], -first[..., :half]], axis=2)
    cross_re = jnp.einsum("fik,fjk->fij", first, second, preferred_element_type=jnp.float32)
    cross_im = jnp.einsum("fik,fjk->fij", turned, second, preferred_element_type=jnp.float32)
    return (cross_re, cross_im)


def lag_block(cross_re, cross_im, inverse, low, high):
    stacked = (jnp.concatenate([cross_re, cross_im], axis=0) / math.sqrt(NW)).astype(jnp.bfloat16)
    table = jnp.concatenate([inverse[low:high], inverse[F + low : F + high]], axis=0)
    return lax.dot_general(
        stacked, table, (((0,), (0,)), ((), ())), preferred_element_type=jnp.float32
    )


def on_device(traces, live_flags):
    forward, taper, near, counts, inverse = make_tables()
    white = whiten(traces, live_flags, forward, taper, near, counts)
    per_dev = white.shape[1]
    width = F // 4
    first = lax.all_gather(white, "col", axis=1, tiled=True)
    second = lax.all_gather(white, "row", axis=1, tiled=True)
    pairs = (first, second)
    rows = pairs[0].shape[1]
    cols = pairs[1].shape[1]
    corr = jnp.zeros((rows, cols, LAGS), jnp.float32)
    for block in range(4):
        low = block * width
        high = low + width
        cross_re = None
        cross_im = None
        first, second = pairs
        part_re, part_im = cross_terms(first[low:high], second[low:high])
        cross_re = part_re
        cross_im = part_im
        corr = corr + lag_block(cross_re, cross_im, inverse, low, high)
    corr = corr / math.sqrt(F)
    n_col = lax.axis_size("col")
    chan_i = lax.axis_index("row") * rows + jnp.arange(rows, dtype=jnp.int32)
    local_j = jnp.arange(cols, dtype=jnp.int32)
    chan_j = (local_j // per_dev * n_col + lax.axis_index("col")) * per_dev + local_j % per_dev
    same = chan_i[:, None] == chan_j[None, :]
    corr = jnp.where(same[:, :, None], 0.0, corr)
    return corr.astype(jnp.bfloat16)


def solution(mesh):
    in_specs = (P(("row", "col"), None, None), P(("row", "col")))
    out_specs = P("row", "col", None)
    return jax.shard_map(
        on_device, mesh=mesh, in_specs=in_specs, out_specs=out_specs, check_vma=False
    )
```

profile of v0, /device:TPU:0, one launch (start us, length us, event | category | flops | bytes accessed | tf_op | source)
XLA Modules:
  0.0 1218.0 jit_solution(2465586422324349981)
XLA Ops:
  6.5 0.0 all-gather.3.cloned.1.call-start
  6.5 2.1 sine_negate_fusion
  8.7 0.5 convert_reduce_fusion
  9.2 3.4 convert_multiply_fusion
  12.6 14.1 %fusion.50 = f32[4096,512]{0,1:T(8,128)S(1)} fusion(f32[4096,512]{1,0:T(8,128)S(1)} %bitcast.21, f32[512,256]{1,0:T(8,128)S(1)} %get-tuple-element.33, f32[512,256]{1,0:T(8,128)S(1)} %get-tuple-element.34), kind=kOutput, calls=%fused_computation.64 | convolution fusion | flops 12885164032 | bytes 17825792 | tf_op jit(solution)/shard_map/dot_general | solution.py:33
  26.7 0.8 fusion.54
  27.6 3.6 slice_multiply_fusion.1
  31.2 3.9 pad_maximum_fusion
  35.2 9.1 copy.29
  44.2 10.7 concatenate.48
  55.0 0.0 copy-done.15
  55.0 9.8 fusion.49
  64.8 5.1 copy.30
  69.9 6.4 copy.31
  76.3 0.0 all-gather.3.cloned.1.call-update
  76.3 0.0 all-gather.5.cloned.1.call-start
  76.4 0.7 all-gather.5.cloned.1.call-update
  77.1 0.5 cosine_convert_fusion
  77.6 0.8 broadcast_compare_fusion
  78.4 0.7 fusion.101
  79.1 286.8 %all-gather.3.cloned.1.call-done = bf16[256,256,128]{2,0,1:T(8,128)(2,1)} async-done(((bf16[256,64,128]{2,0,1:T(8,128)(2,1)}), bf16[256,256,128]{2,0,1:T(8,128)(2,1)}) %all-gather.3.cloned.1.call-update) | async-done | bytes 16777232 | tf_op jit(solution)/shard_map/all_gather | solution.py:68
  366.0 26.9 %fusion.100 = (bf16[64,256,64]{2,0,1:T(8,128)(2,1)}, bf16[64,256,64]{2,0,1:T(8,128)(2,1)}, bf16[64,256,64]{2,0,1:T(8,128)(2,1)S(1)}, bf16[64,256,64]{2,0,1:T(8,1...) fusion(bf16[256,256,128]{2,0,1:T(8,128)(2,1)} %all-gather.3.clo, ...), kind=kLoop, calls=%fused_computation.138 | loop fusion | bytes 33554432 | tf_op jit(solution)/shard_map/slice | solution.py:49
  392.9 0.0 copy-start.5
  392.9 0.0 copy-start.4
  392.9 7.0 copy.59
  399.9 0.0 copy-done.5
  399.9 4.7 copy.55
  404.6 0.0 copy-done.4
  404.6 4.7 copy.63
  409.3 0.0 copy-done.3
  409.3 4.8 copy.67
  414.1 0.0 copy-done.2
  414.1 10.4 copy_negate_fusion.2
  424.5 0.0 copy-done.1
  424.5 11.4 copy_negate_fusion.3
  435.9 10.6 copy_negate_fusion.1
  446.5 0.0 copy-done
  446.5 10.2 copy_negate_fusion
  456.8 0.0 slice-done
  456.8 0.0 slice-done.1
  456.8 0.0 slice-done.3
  456.8 7.0 fusion.99
  463.7 63.1 %all-gather.5.cloned.1.call-done = bf16[256,512,128]{2,0,1:T(8,128)(2,1)} async-done(((bf16[256,64,128]{2,0,1:T(8,128)(2,1)}), bf16[256,512,128]{2,0,1:T(8,128)(2,1)}) %all-gather.5.cloned.1.call-update) | async-done | bytes 33554448 | tf_op jit(solution)/shard_map/all_gather | solution.py:69
  526.9 22.8 %fusion.98 = (bf16[64,512,128]{2,0,1:T(8,128)(2,1)}, bf16[64,512,128]{2,0,1:T(8,128)(2,1)}, bf16[64,512,128]{2,0,1:T(8,128)(2,1)}, bf16[64,512,128]{2,0,1:T(8,128)(2,1)}) fusion(bf16[256,512,128]{2,0,1:T(8,128)(2,1)} %all-gather.5.cloned.1.call-done), kind=kLoop, calls=%fused_computation.136 | loop fusion | bytes 67108864 | tf_op jit(solution)/shard_map/slice | solution.py:80
  549.7 27.0 %fusion.24 = f32[64,256,512]{2,1,0:T(8,128)} fusion(bf16[64,512,128]{2,0,1:T(8,128)(2,1)} %get-tuple-element.7, bf16[64,256,128]{2,0,1:T(8,128)(2,1)} %get-tuple-element.12), kind=kOutput, calls=%fused_computation.30 | convolution fusion | flops 2147483648 | bytes 46137344 | tf_op jit(solution)/shard_map/fik,fjk->fij/dot_general | solution.py:50
  576.7 20.5 %fusion.22 = f32[64,256,512]{2,1,0:T(8,128)} fusion(bf16[64,512,128]{2,0,1:T(8,128)(2,1)} %get-tuple-element.7, bf16[64,256,64]{2,1,0:T(8,128)(2,1)} %copy_negate_fusion.2, bf16[64,256,64]{2,1,0:T(8,128)(2,1)} %copy.59), kind=kOutput, calls=%fused_computation.28 | convolution fusion | flops 2155872256 | bytes 46137344 | tf_op jit(solution)/shard_map/fik,fjk->fij/dot_general | solution.py:51
  597.2 32.9 %fusion.1 = bf16[128,256,512]{2,1,0:T(8,128)(2,1)} fusion(f32[64,256,512]{2,1,0:T(8,128)} %fusion.22, f32[64,256,512]{2,1,0:T(8,128)} %fusion.24), kind=kLoop, calls=%fused_computation.3 | loop fusion | flops 50331648 | bytes 100663296 | tf_op jit(solution)/shard_map/convert_element_type | solution.py:56
  630.2 27.4 %fusion.28 = f32[64,256,512]{2,1,0:T(8,128)} fusion(bf16[64,512,128]{2,0,1:T(8,128)(2,1)} %get-tuple-element.5, bf16[64,256,128]{2,0,1:T(8,128)(2,1)} %get-tuple-element.9), kind=kOutput, calls=%fused_computation.34 | convolution fusion | flops 2147483648 | bytes 46137344 | tf_op jit(solution)/shard_map/fik,fjk->fij/dot_general | solution.py:50
  657.6 20.7 %fusion.26 = f32[64,256,512]{2,1,0:T(8,128)} fusion(bf16[64,512,128]{2,0,1:T(8,128)(2,1)} %get-tuple-element.5, bf16[64,256,64]{2,1,0:T(8,128)(2,1)} %copy_negate_fusion.3, bf16[64,256,64]{2,1,0:T(8,128)(2,1)} %copy.55), kind=kOutput, calls=%fused_computation.32 | convolution fusion | flops 2155872256 | bytes 46137344 | tf_op jit(solution)/shard_map/fik,fjk->fij/dot_general | solution.py:51
  678.3 33.0 %fusion = bf16[128,256,512]{2,1,0:T(8,128)(2,1)} fusion(f32[64,256,512]{2,1,0:T(8,128)} %fusion.26, f32[64,256,512]{2,1,0:T(8,128)} %fusion.28), kind=kLoop, calls=%fused_computation.1 | loop fusion | flops 50331648 | bytes 100663296 | tf_op jit(solution)/shard_map/convert_element_type | solution.py:56
  711.2 26.9 %fusion.20 = f32[64,256,512]{2,1,0:T(8,128)} fusion(bf16[64,512,128]{2,0,1:T(8,128)(2,1)} %get-tuple-element.6, bf16[64,256,128]{2,0,1:T(8,128)(2,1)} %get-tuple-element.11), kind=kOutput, calls=%fused_computation.26 | convolution fusion | flops 2147483648 | bytes 46137344 | tf_op jit(solution)/shard_map/fik,fjk->fij/dot_general | solution.py:50
  738.2 20.5 %fusion.18 = f32[64,256,512]{2,1,0:T(8,128)} fusion(bf16[64,512,128]{2,0,1:T(8,128)(2,1)} %get-tuple-element.6, bf16[64,256,64]{2,1,0:T(8,128)(2,1)} %copy_negate_fusion.1, bf16[64,256,64]{2,1,0:T(8,128)(2,1)} %copy.63), kind=kOutput, calls=%fused_computation.24 | convolution fusion | flops 2155872256 | bytes 46137344 | tf_op jit(solution)/shard_map/fik,fjk->fij/dot_general | solution.py:51
  758.7 32.9 %fusion.2 = bf16[128,256,512]{2,1,0:T(8,128)(2,1)} fusion(f32[64,256,512]{2,1,0:T(8,128)} %fusion.18, f32[64,256,512]{2,1,0:T(8,128)} %fusion.20), kind=kLoop, calls=%fused_computation.5 | loop fusion | flops 50331648 | bytes 100663296 | tf_op jit(solution)/shard_map/convert_element_type | solution.py:56
  791.6 27.4 %fusion.16 = f32[64,256,512]{2,1,0:T(8,128)} fusion(bf16[64,512,128]{2,0,1:T(8,128)(2,1)} %get-tuple-element.8, bf16[64,256,128]{2,0,1:T(8,128)(2,1)} %get-tuple-element.10), kind=kOutput, calls=%fused_computation.22 | convolution fusion | flops 2147483648 | bytes 46137344 | tf_op jit(solution)/shard_map/fik,fjk->fij/dot_general | solution.py:50
  819.0 20.5 %fusion.14 = f32[64,256,512]{2,1,0:T(8,128)} fusion(bf16[64,512,128]{2,0,1:T(8,128)(2,1)} %get-tuple-element.8, bf16[64,256,64]{2,1,0:T(8,128)(2,1)} %copy_negate_fusion, bf16[64,256,64]{2,1,0:T(8,128)(2,1)} %copy.67), kind=kOutput, calls=%fused_computation.20 | convolution fusion | flops 2155872256 | bytes 46137344 | tf_op jit(solution)/shard_map/fik,fjk->fij/dot_general | solution.py:51
  839.5 32.9 %fusion.3 = bf16[128,256,512]{2,1,0:T(8,128)(2,1)} fusion(f32[64,256,512]{2,1,0:T(8,128)} %fusion.14, f32[64,256,512]{2,1,0:T(8,128)} %fusion.16), kind=kLoop, calls=%fused_computation.7 | loop fusion | flops 50331648 | bytes 100663296 | tf_op jit(solution)/shard_map/convert_element_type | solution.py:56
  872.5 79.5 %fusion.8 = f32[256,512,128]{2,1,0:T(8,128)} fusion(bf16[128,256,512]{2,1,0:T(8,128)(2,1)} %fusion.1, bf16[64,128]{1,0:T(8,128)(2,1)S(1)} %copy-done.14, bf16[64,128]{1,0:T(8,128)(2,1)S(1)} %copy-done.13), kind=kOutput, calls=%fused_computation.13 | convolution fusion | flops 4295032832 | bytes 100696064 | tf_op jit(solution)/shard_map/dot_general | solution.py:58
  952.0 0.0 copy-done.12
  952.1 79.6 %fusion.6 = f32[256,512,128]{2,1,0:T(8,128)} fusion(bf16[128,256,512]{2,1,0:T(8,128)(2,1)} %fusion.2, bf16[64,128]{1,0:T(8,128)(2,1)S(1)} %copy-done.12, bf16[64,128]{1,0:T(8,128)(2,1)S(1)} %copy-done.11), kind=kOutput, calls=%fused_computation.11 | convolution fusion | flops 4295032832 | bytes 100696064 | tf_op jit(solution)/shard_map/dot_general | solution.py:58
  1031.6 0.0 copy-done.10
  1031.6 92.6 %fusion.4 = f32[256,512,128]{2,1,0:T(8,128)} fusion(bf16[128,256,512]{2,1,0:T(8,128)(2,1)} %fusion.3, bf16[64,128]{1,0:T(8,128)(2,1)S(1)} %copy-done.10, bf16[64,128]{1,0:T(8,128)(2,1)S(1)} %copy-done.9), kind=kOutput, calls=%fused_computation.9 | convolution fusion | flops 4295032832 | bytes 100696064 | tf_op jit(solution)/shard_map/dot_general | solution.py:58
  1124.2 0.0 copy-done.6
  1124.2 0.0 copy-done.8
  1124.3 86.8 %select_convert_fusion = bf16[256,512,128]{2,1,0:T(8,128)(2,1)} fusion(f32[256,512,128]{2,1,0:T(8,128)} %fusion.4, f32[256,512,128]{2,1,0:T(8,128)} %fusion.6, f32[256,512,128]{2,1,0:T(8,128)} %fusion.8, pred[256,512]{1,0:T(8,128)(4,1)S(1)} %copy-done.6, bf16[128,256,512]{2,1,0:T(8,128)(2,1)} %fusion, bf16[64,128]{1,0:T(8,128)(2,1)S(1)} %copy-done.8, ...), kind=kOutput, calls=%fused_computation.8 | convolution fusion | flops 4395696128 | bytes 268599296 | tf_op jit(solution)/shard_map/dot_general | solution.py:58
  (31 shorter events, 0.1 us)
Async XLA Ops:
  6.5 359.4 %all-gather.3.cloned.1.call-start = ((), (), s32[]{:S(2)}) async-start(), calls=%async_computation | async-start | bytes 20971520 | tf_op jit(solution)/shard_map/all_gather | solution.py:68
  44.2 10.7 copy-start.15
  76.3 450.6 %all-gather.5.cloned.1.call-start = ((), (), s32[]{:S(2)}) async-start(), calls=%async_computation.1 | async-start | bytes 37748736 | tf_op jit(solution)/shard_map/all_gather | solution.py:69
  392.9 7.0 copy-start.5
  392.9 11.7 copy-start.4
  399.9 9.4 copy-start.3
  404.6 9.5 copy-start.2
  409.3 15.2 %copy-start.1 = (bf16[64,256,64]{2,0,1:T(8,128)(2,1)S(1)}, bf16[64,256,64]{2,0,1:T(8,128)(2,1)}, u32[]{:S(2)}) copy-start(bf16[64,256,64]{2,0,1:T(8,128)(2,1)} %get-tuple-element.19) | copy-start | bytes 6291460
  414.1 42.7 %slice-start = ((s8[16777216]{0:T(1024)(128)(4,1)}), s8[4194304]{0:T(1024)(128)(4,1)S(1)}, s32[]{:S(2)}) async-start(s8[16777216]{0:T(1024)(128)(4,1)} %bitcast.19), calls=%async_computation.2 | async-start | bytes 8388608
  424.5 32.3 %slice-start.1 = ((s8[16777216]{0:T(1024)(128)(4,1)}), s8[4194304]{0:T(1024)(128)(4,1)S(1)}, s32[]{:S(2)}) async-start(s8[16777216]{0:T(1024)(128)(4,1)} %bitcast.19), calls=%async_computation.3 | async-start | bytes 8388608
  424.5 22.0 %copy-start = (bf16[64,256,64]{2,0,1:T(8,128)(2,1)S(1)}, bf16[64,256,64]{2,0,1:T(8,128)(2,1)}, u32[]{:S(2)}) copy-start(bf16[64,256,64]{2,0,1:T(8,128)(2,1)} %get-tuple-element.20) | copy-start | bytes 6291460
  435.9 20.9 %slice-start.2 = ((s8[16777216]{0:T(1024)(128)(4,1)}), s8[4194304]{0:T(1024)(128)(4,1)S(1)}, s32[]{:S(2)}) async-start(s8[16777216]{0:T(1024)(128)(4,1)} %bitcast.19), calls=%async_computation.4 | async-start | bytes 8388608
  446.5 10.3 slice-start.3
  839.5 32.9 %copy-start.13 = (bf16[64,128]{1,0:T(8,128)(2,1)S(1)}, bf16[64,128]{1,0:T(8,128)(2,1)}, u32[]{:S(2)}) copy-start(bf16[64,128]{1,0:T(8,128)(2,1)} %get-tuple-element.26) | copy-start | bytes 49156
  839.5 32.9 %copy-start.14 = (bf16[64,128]{1,0:T(8,128)(2,1)S(1)}, bf16[64,128]{1,0:T(8,128)(2,1)}, u32[]{:S(2)}) copy-start(bf16[64,128]{1,0:T(8,128)(2,1)} %get-tuple-element.35) | copy-start | bytes 49156
  872.5 79.5 %copy-start.11 = (bf16[64,128]{1,0:T(8,128)(2,1)S(1)}, bf16[64,128]{1,0:T(8,128)(2,1)}, u32[]{:S(2)}) copy-start(bf16[64,128]{1,0:T(8,128)(2,1)} %get-tuple-element.25) | copy-start | bytes 49156
  872.5 79.5 %copy-start.12 = (bf16[64,128]{1,0:T(8,128)(2,1)S(1)}, bf16[64,128]{1,0:T(8,128)(2,1)}, u32[]{:S(2)}) copy-start(bf16[64,128]{1,0:T(8,128)(2,1)} %get-tuple-element.36) | copy-start | bytes 49156
  952.0 79.6 %copy-start.9 = (bf16[64,128]{1,0:T(8,128)(2,1)S(1)}, bf16[64,128]{1,0:T(8,128)(2,1)}, u32[]{:S(2)}) copy-start(bf16[64,128]{1,0:T(8,128)(2,1)} %get-tuple-element.24) | copy-start | bytes 49156
  952.1 79.6 %copy-start.10 = (bf16[64,128]{1,0:T(8,128)(2,1)S(1)}, bf16[64,128]{1,0:T(8,128)(2,1)}, u32[]{:S(2)}) copy-start(bf16[64,128]{1,0:T(8,128)(2,1)} %get-tuple-element.37) | copy-start | bytes 49156
  1031.6 92.6 %copy-start.6 = (pred[256,512]{1,0:T(8,128)(4,1)S(1)}, pred[256,512]{1,0:T(8,128)(4,1)}, u32[]{:S(2)}) copy-start(pred[256,512]{1,0:T(8,128)(4,1)} %broadcast_compare_fusion) | copy-start | bytes 393220
  1031.6 92.6 %copy-start.7 = (bf16[64,128]{1,0:T(8,128)(2,1)S(1)}, bf16[64,128]{1,0:T(8,128)(2,1)}, u32[]{:S(2)}) copy-start(bf16[64,128]{1,0:T(8,128)(2,1)} %get-tuple-element.23) | copy-start | bytes 49156
  1031.6 92.6 %copy-start.8 = (bf16[64,128]{1,0:T(8,128)(2,1)S(1)}, bf16[64,128]{1,0:T(8,128)(2,1)}, u32[]{:S(2)}) copy-start(bf16[64,128]{1,0:T(8,128)(2,1)} %get-tuple-element.38) | copy-start | bytes 49156
Sparse Core Ops, SparseCore 0:
  76.4 289.4 all-gather.2
  367.8 158.9 all-gather.4
where the time goes:
time: 1220 us
  matrix products  547 us (45%)
  waiting for transfers between devices  351 us (29%)
  other arithmetic  196 us (16%)
  local copies, waits for them, and re-layouts  110 us (9%)
  between operations  13.8 us (1%)
    dot_general x4, matrix products, lag_block(): lax.dot_general(stacked, table, (((0,), (0,)), ((), ())), preferred_eleme...  338 us
    all_gather x1, waiting for transfers between devices, on_device(): first = lax.all_gather(white, 'col', axis=1, tiled=True)  287 us
    convert_element_type x4, other arithmetic, lag_block(): (jnp.concatenate([cross_re, cross_im], axis=0) / math.sqrt(NW)).astype(jn...  132 us
    dot_general x4, matrix products, cross_terms(): jnp.einsum('fik,fjk->fij', first, second, preferred_element_type=jnp.floa...  109 us
    dot_general x4, matrix products, cross_terms(): jnp.einsum('fik,fjk->fij', turned, second, preferred_element_type=jnp.flo...  82.2 us
    all_gather x1, waiting for transfers between devices, on_device(): second = lax.all_gather(white, 'row', axis=1, tiled=True)  63.1 us
    neg x4, other arithmetic, cross_terms(): turned = jnp.concatenate([first[..., half:], -first[..., :half]], axis=2)  42.7 us
    slice x2, local copies, waits for them, and re-layouts, on_device(): part_re, part_im = cross_terms(first[low:high], second[low:high])  29.8 us
  transfers between devices with their start and end apart: 2, of which 2 were waited for; matrix products, arithmetic and copies ran while one was open for 8% of the time, Pallas kernels for 0%

commit v1 on v0

v1 whole, which is shorter than its diff:
```python
import functools
import math

import jax
import jax.numpy as jnp
from jax import lax
from jax.experimental import pallas as pl
from jax.experimental.pallas import tpu as pltpu
from jax.sharding import PartitionSpec as P

F = 256
LAGS = 128
SAMP = 512
NW = 64


def make_tables():
    samples = jnp.arange(SAMP, dtype=jnp.int32)
    bins = jnp.arange(F, dtype=jnp.int32)
    phase = samples[:, None] * bins[None, :] % SAMP
    angle = 2.0 * math.pi * phase.astype(jnp.float32) / SAMP
    forward = jnp.concatenate([jnp.cos(angle), -jnp.sin(angle)], axis=1)
    taper = 0.5 - 0.5 * jnp.cos(2.0 * math.pi * samples.astype(jnp.float32) / SAMP)
    near = (jnp.abs(bins[:, None] - bins[None, :]) <= 4).astype(jnp.float32)
    counts = jnp.sum(near, axis=0)
    lagval = jnp.arange(LAGS, dtype=jnp.int32) - LAGS // 2
    lphase = bins[:, None] * lagval[None, :] % SAMP
    langle = 2.0 * math.pi * lphase.astype(jnp.float32) / SAMP
    inverse = jnp.concatenate([jnp.cos(langle), -jnp.sin(langle)], axis=0).astype(jnp.bfloat16)
    return (forward, taper, near, counts, inverse)


def whiten(traces, live_flags, forward, taper, near, counts):
    chans = traces.shape[0]
    tapered = traces.astype(jnp.float32) * taper
    spectra = jnp.dot(tapered.reshape(-1, SAMP), forward, precision=lax.Precision.HIGHEST)
    real_part = spectra[:, :F]
    imag_part = spectra[:, F:]
    power = real_part * real_part + imag_part * imag_part
    smooth = jnp.dot(power, near, precision=lax.Precision.HIGHEST) / counts
    level = jnp.mean(power, axis=1, keepdims=True)
    scale = 1.0 / jnp.sqrt(smooth + 0.05 * level + 1e-06)
    alive = jnp.repeat(live_flags.astype(jnp.float32), NW)[:, None]
    real_white = (real_part * scale * alive).astype(jnp.bfloat16)
    imag_white = (imag_part * scale * alive).astype(jnp.bfloat16)
    real_white = jnp.transpose(real_white.reshape(chans, NW, F), (2, 0, 1))
    imag_white = jnp.transpose(imag_white.reshape(chans, NW, F), (2, 0, 1))
    return jnp.concatenate([real_white, imag_white], axis=2)


def slab_kernel(n_parts, n_f, fb, ib, has_out, base_ref, *refs):
    parts = refs[:n_parts]
    second_ref, table_ref, chan_j_ref = refs[n_parts : n_parts + 3]
    out_ref, scratch = refs[-2:]
    step = pl.program_id(1)
    rows = sum(part.shape[1] for part in parts)

    @pl.when(step < n_f)
    def _():
        lane = lax.broadcasted_iota(jnp.int32, (rows, 2 * NW), 1)
        sign = jnp.where(lane < NW, 1.0, -1.0)
        for b in range(fb):
            pieces = [part[b] for part in parts]
            first = pieces[0] if n_parts == 1 else jnp.concatenate(pieces, axis=0)
            turned = (pltpu.roll(first.astype(jnp.float32), NW, 1) * sign).astype(jnp.bfloat16)
            both = jnp.concatenate([first, turned], axis=0)
            cross = lax.dot_general(
                both, second_ref[b], (((1,), (1,)), ((), ())), preferred_element_type=jnp.float32
            )
            at = step * fb + b
            for c in range(scratch.shape[0]):
                lanes = slice(c * 128, (c + 1) * 128)
                scratch[c, pl.ds(at, rows, stride=2 * F), :] = cross[:rows, lanes]
                scratch[c, pl.ds(at + F, rows, stride=2 * F), :] = cross[rows:, lanes]

    @pl.when(step >= n_f)
    def _():
        group = step - n_f
        chan_j = chan_j_ref[...]
        for r in range(ib):
            start = pl.multiple_of((group * ib + r) * (2 * F), 2 * F)
            for c in range(scratch.shape[0]):
                stacked = scratch[c, pl.ds(start, 2 * F), :].astype(jnp.bfloat16)
                corr = jnp.dot(table_ref[...], stacked, preferred_element_type=jnp.float32)
                chan_i = base_ref[base_ref.shape[0] - 1] + base_ref[group] * ib + r
                keep = jnp.where(chan_j[:, c * 128 : (c + 1) * 128] == chan_i, 0.0, SCALE)
                corr = jnp.transpose(corr * keep)
                out_ref[r, c * 128 : (c + 1) * 128, :] = corr.astype(jnp.bfloat16)


def slab(parts, second, table, chan_j, base, total_rows, out):
    rows = sum(part.shape[1] for part in parts)
    cols = second.shape[1]
    ib, fb = 8, 16
    jt = min(256, cols)
    n_f, n_i = F // fb, rows // ib
    f_of = lambda p: jnp.minimum(p, n_f - 1)
    in_specs = [
        pl.BlockSpec((fb, part.shape[1], 2 * NW), lambda j, p, s: (f_of(p), 0, 0))
        for part in parts
    ]
    in_specs += [
        pl.BlockSpec((fb, jt, 2 * NW), lambda j, p, s: (f_of(p), j, 0)),
        pl.BlockSpec((LAGS, 2 * F), lambda j, p, s: (0, 0)),
        pl.BlockSpec((1, jt), lambda j, p, s: (0, j)),
    ]
    args = [*parts, second, table, chan_j]
    aliases = {}
    if out is not None:
        in_specs.append(pl.BlockSpec(memory_space=pl.ANY))
        aliases = {1 + len(args): 0}
        args.append(out)
    return pl.pallas_call(
        functools.partial(slab_kernel, len(parts), n_f, fb, ib, out is not None),
        out_shape=jax.ShapeDtypeStruct((total_rows, cols, LAGS), jnp.bfloat16),
        grid_spec=pltpu.PrefetchScalarGridSpec(
            num_scalar_prefetch=1,
            grid=(cols // jt, n_f + n_i),
            in_specs=in_specs,
            out_specs=pl.BlockSpec(
                (ib, jt, LAGS), lambda j, p, s: (s[jnp.maximum(p - n_f, 0)], j, 0)
            ),
            scratch_shapes=[pltpu.VMEM((jt // 128, rows * 2 * F, 128), jnp.float32)],
        ),
        input_output_aliases=aliases,
        compiler_params=pltpu.CompilerParams(
            dimension_semantics=("arbitrary", "arbitrary"), vmem_limit_bytes=52 * 2**20
        ),
        cost_estimate=pl.CostEstimate(
            flops=rows * cols * F * 4 * (2 * NW + LAGS) * 2,
            bytes_accessed=second.size * 2 + rows * cols * LAGS * 2,
            transcendentals=0,
        ),
    )(base, *args)


SCALE = 1.0 / (math.sqrt(NW) * math.sqrt(F))


def on_device(traces, live_flags):
    forward, taper, near, counts, inverse = make_tables()
    white = whiten(traces, live_flags, forward, taper, near, counts)
    per_dev = white.shape[1]
    n_col = lax.axis_size("col")
    me = lax.axis_index("col")
    rows = per_dev * n_col
    second = lax.all_gather(white, "row", axis=1, tiled=True)
    cols = second.shape[1]
    table = jnp.transpose(inverse)
    local_j = jnp.arange(cols, dtype=jnp.int32)
    chan_j = ((local_j // per_dev * n_col + me) * per_dev + local_j % per_dev)[None, :]
    offset = lax.axis_index("row").astype(jnp.int32)[None] * rows
    half = per_dev // 2
    if half % 16 != 0:
        first = lax.all_gather(white, "col", axis=1, tiled=True)
        base = jnp.concatenate([jnp.arange(rows // 8, dtype=jnp.int32), offset])
        return slab([first], second, table, chan_j, base, rows, None)
    ahead, behind = white[:, :half], white[:, half:]
    up = [(s, (s + 1) % n_col) for s in range(n_col)]
    down = [(s, (s - 1) % n_col) for s in range(n_col)]
    groups = jnp.arange(half // 8, dtype=jnp.int32)
    out = None
    for k in range(n_col):
        source_a = (me - k) % n_col
        source_b = (me + k) % n_col
        base = jnp.concatenate(
            [source_a * (per_dev // 8) + groups, (source_b * per_dev + half) // 8 + groups, offset]
        ).astype(jnp.int32)
        parts = [ahead, behind]
        if k < n_col - 1:
            ahead = lax.ppermute(ahead, "col", up)
            behind = lax.ppermute(behind, "col", down)
        out = slab(parts, second, table, chan_j, base, rows, out)
    return out


def solution(mesh):
    in_specs = (P(("row", "col"), None, None), P(("row", "col")))
    out_specs = P("row", "col", None)
    return jax.shard_map(
        on_device, mesh=mesh, in_specs=in_specs, out_specs=out_specs, check_vma=False
    )
```

time: 1220 us -> 592 us (0.49)
  matrix products: 547 us -> 23.2 us
  Pallas kernels: 0 us -> 332 us
  other arithmetic: 196 us -> 18 us
  waiting for transfers between devices: 351 us -> 179 us
  local copies, waits for them, and re-layouts: 110 us -> 17 us
    dot_general x12 -> x0, matrix products: 529 us -> none  [the longest x4 338 us: lag_block(): lax.dot_general(stacked, table, (((0,), (0,)), ((), ())), preferred_eleme...]
    pallas_call x0 -> x4, Pallas kernels: none -> 332 us  [slab(): pl.pallas_call(functools.partial(slab_kernel, len(parts), n_f, fb, ib, ou...]
    all_gather x1 -> x0, waiting for transfers between devices: 287 us -> none  [on_device(): first = lax.all_gather(white, 'col', axis=1, tiled=True)]
    ppermute x0 -> x6, waiting for transfers between devices: none -> 179 us  [the longest x3 90.6 us: on_device(): ahead = lax.ppermute(ahead, 'col', up)]
    convert_element_type x5 -> x0, other arithmetic: 142 us -> none  [the longest x4 132 us: lag_block(): (jnp.concatenate([cross_re, cross_im], axis=0) / math.sqrt(NW)).astype(jn...]
    all_gather x1, waiting for transfers between devices: 63.1 us -> 0.01 us  [on_device(): second = lax.all_gather(white, 'row', axis=1, tiled=True)]
    slice x4 -> x0, local copies, waits for them, and re-layouts: 57.3 us -> none  [the longest x2 29.8 us: on_device(): part_re, part_im = cross_terms(first[low:high], second[low:high])]
    neg x4 -> x0, other arithmetic: 42.7 us -> none  [cross_terms(): turned = jnp.concatenate([first[..., half:], -first[..., :half]], axis=2)]
  transfers between devices with their start and end apart: 2 -> 7, of which waited for: 2 -> 4; matrix products, arithmetic and copies ran while one was open for 8% -> 1% of each run, Pallas kernels for 0% -> 42%
where the time goes in v1:
time: 592 us; the launch traced here: 591 us
  Pallas kernels  332 us (56%)
  waiting for transfers between devices  179 us (30%)
  matrix products  23.2 us (4%)
  other arithmetic  18 us (3%)
  local copies, waits for them, and re-layouts  17 us (3%)
  between operations  13.5 us (2%)
  starting transfers between devices  8.34 us (1%)
    pallas_call x4, Pallas kernels, slab(): pl.pallas_call(functools.partial(slab_kernel, len(parts), n_f, fb, ib, ou...  332 us
    ppermute x3, waiting for transfers between devices, on_device(): ahead = lax.ppermute(ahead, 'col', up)  90.6 us
    ppermute x3, waiting for transfers between devices, on_device(): behind = lax.ppermute(behind, 'col', down)  88.6 us
    dot_general x1, matrix products, whiten(): jnp.dot(tapered.reshape(-1, SAMP), forward, precision=lax.Precision.HIGHEST)  14.6 us
  transfers between devices with their start and end apart: 7, of which 4 were waited for; matrix products, arithmetic and copies ran while one was open for 1% of the time, Pallas kernels for 42%

profile of v1, /device:TPU:0, one launch (start us, length us, event | category | flops | bytes accessed | tf_op | source)
XLA Modules:
  0.0 591.0 jit_solution(2475471522752446426)
XLA Ops:
  6.5 0.0 all-gather.2.cloned.1.call-start
  6.5 2.1 sine_negate_fusion
  8.7 0.2 convert_reduce_fusion
  8.9 3.4 convert_multiply_fusion
  12.3 14.6 %fusion.5 = f32[4096,512]{1,0:T(8,128)S(1)} fusion(f32[4096,512]{1,0:T(8,128)S(1)} %bitcast.13, f32[512,256]{1,0:T(8,128)S(1)} %get-tuple-element.13, f32[512,256]{1,0:T(8,128)S(1)} %get-tuple-element.14), kind=kOutput, calls=%fused_computation.15 | convolution fusion | flops 12885164032 | bytes 17825792 | tf_op jit(solution)/shard_map/dot_general | solution.py:36
  27.0 0.0 copy-start
  27.0 0.0 copy-start.3
  27.0 0.6 fusion.9
  27.7 2.7 copy-done
  30.4 0.0 copy-done.3
  30.4 0.1 broadcast_in_dim.2
  30.5 0.1 mul.168
  30.6 8.6 %multiply_convert_fusion = (bf16[4096,256]{1,0:T(8,128)(2,1)S(1)}, bf16[4096,256]{1,0:T(8,128)(2,1)}) fusion(f32[4096,512]{1,0:T(8,128)} %copy-done, f32[4096]{0:T(1024)S(1)} %mul.168, f32[4096]{0:T(1024)S(1)} %broadcast_multiply_fusion, f32[256]{0:T(256)S(1)} %convert_reduce_fusion), kind=kOutput, calls=%fused_computation.5 | convolution fusion | flops 3234004992 | bytes 21005312 | tf_op jit(solution)/shard_map/dot_general | solution.py:40
  39.1 7.4 %copy.10 = bf16[64,64,256]{1,0,2:T(8,128)(2,1)} copy(bf16[64,64,256]{2,1,0:T(8,128)(2,1)} %bitcast.15) | data formatting | bytes 4194304 | tf_op jit(solution)/shard_map/reshape | solution.py:46
  46.5 6.7 %copy.11 = bf16[64,64,256]{1,0,2:T(8,128)(2,1)} copy(bf16[64,64,256]{2,1,0:T(8,128)(2,1)S(1)} %bitcast.14) | data formatting | bytes 4194304 | tf_op jit(solution)/shard_map/reshape | solution.py:47
  53.2 6.0 %pad_maximum_fusion = bf16[256,64,128]{2,1,0:T(8,128)(2,1)} fusion(bf16[256,64,64]{2,1,0:T(8,128)(2,1)} %bitcast.11, bf16[256,64,64]{2,1,0:T(8,128)(2,1)} %bitcast.9), kind=kLoop, calls=%fused_computation.10 | loop fusion | flops 8388608 | bytes 8388608 | tf_op jit(solution)/shard_map/concatenate | solution.py:48
  59.2 0.0 all-gather.2.cloned.1.call-update
  59.2 4.7 fusion.4
  63.9 0.0 copy-start.2
  63.9 0.0 copy-start.1
  63.9 3.1 collective-permute-start
  67.0 2.1 collective-permute-start.3
  69.1 46.5 %collective-permute-done.refs_0_ = bf16[256,32,128]{2,1,0:T(8,128)(2,1)} collective-permute-done((bf16[256,32,128]{2,1,0:T(8,128)(2,1)S(1)}, bf16[256,32,128]{2,1,0:T(8,128)(2,1)}, u32[]{:S(2)}, u32[]{:S(2)}) %collective-permute-start) | collective-permute-done | bytes 2097184 | tf_op jit(solution)/shard_map/ppermute | solution.py:171
  115.7 0.0 collective-permute-start.1
  115.7 43.7 %collective-permute-done.3.refs_1_ = bf16[256,32,128]{2,1,0:T(8,128)(2,1)} collective-permute-done((bf16[256,32,128]{2,1,0:T(8,128)(2,1)S(1)}, bf16[256,32,128]{2,1,0:T(8,128)(2,1)}, u32[]{:S(2)}, u32[]{:S(2)}) %collective-permute-start.3) | collective-permute-done | bytes 2097184 | tf_op jit(solution)/shard_map/ppermute | solution.py:172
  159.4 0.0 copy-done.2
  159.4 3.1 collective-permute-start.4
  162.5 0.1 add_add_fusion.3.base_ref
  162.6 0.1 add_add_fusion.2.base_ref
  162.6 0.1 add_add_fusion
  162.7 0.6 cosine_convert_fusion
  163.4 44.0 %collective-permute-done.1.refs_0_ = bf16[256,32,128]{2,1,0:T(8,128)(2,1)} collective-permute-done((bf16[256,32,128]{2,1,0:T(8,128)(2,1)}, bf16[256,32,128]{2,1,0:T(8,128)(2,1)}, u32[]{:S(2)}, u32[]{:S(2)}) %collective-permute-start.1) | collective-permute-done | bytes 2097184 | tf_op jit(solution)/shard_map/ppermute | solution.py:171
  207.4 0.0 collective-permute-start.2
  207.4 44.9 %collective-permute-done.4.refs_1_ = bf16[256,32,128]{2,1,0:T(8,128)(2,1)} collective-permute-done((bf16[256,32,128]{2,1,0:T(8,128)(2,1)}, bf16[256,32,128]{2,1,0:T(8,128)(2,1)}, u32[]{:S(2)}, u32[]{:S(2)}) %collective-permute-start.4) | collective-permute-done | bytes 2097184 | tf_op jit(solution)/shard_map/ppermute | solution.py:172
  252.3 0.1 collective-permute-start.5
  252.4 0.0 all-gather.2.cloned.1.call-done.refs_2_
  252.4 0.0 copy-done.1
  252.4 83.1 %shard_map.28.refs_5_ = bf16[256,512,128]{2,1,0:T(8,128)(2,1)} custom-call(s32[9]{0:T(128)S(1)} %add_add_fusion.3.base_ref, bf16[256,32,128]{2,1,0:T(8,128)(2,1)} %copy-done.2, bf16[256,32,128]{2,1,0:T(8,128)(2,1)} %copy-done.1, bf16[256,512,128]{2,1,0:T(8,128)(2,1)} %all-gather.2.cloned.1.call-done.refs_2_, ...), custom_call_target="tpu_custom_call" | custom-call | flops 17179869184 | bytes 41943040 | tf_op jit(solution)/shard_map/pallas_call | solution.py:113
  335.5 82.9 %shard_map.29.refs_5_ = bf16[256,512,128]{2,1,0:T(8,128)(2,1)} custom-call(s32[9]{0:T(128)S(1)} %add_add_fusion.2.base_ref, bf16[256,32,128]{2,1,0:T(8,128)(2,1)} %collective-permute-done.refs_0_, bf16[256,32,128]{2,1,0:T(8,128)(2,1)} %collective-permute-done.3.refs_1_, ...), custom_call_target="tpu_custom_call", output_to_operand_aliasing={{}: (6, {})} | custom-call | flops 17179869184 | bytes 41943040 | tf_op jit(solution)/shard_map/pallas_call | solution.py:113
  418.4 82.9 %shard_map.30.refs_5_ = bf16[256,512,128]{2,1,0:T(8,128)(2,1)} custom-call(s32[9]{0:T(128)S(1)} %get-tuple-element.12.base_ref, bf16[256,32,128]{2,1,0:T(8,128)(2,1)} %collective-permute-done.1.refs_0_, bf16[256,32,128]{2,1,0:T(8,128)(2,1)} %collective-permute-done.4.refs_1_, ...), custom_call_target="tpu_custom_call", output_to_operand_aliasing={{}: (6, {})} | custom-call | flops 17179869184 | bytes 41943040 | tf_op jit(solution)/shard_map/pallas_call | solution.py:113
  501.3 0.0 collective-permute-done.2.refs_0_
  501.3 0.0 collective-permute-done.5.refs_1_
  501.3 82.9 %shard_map.31 = bf16[256,512,128]{2,1,0:T(8,128)(2,1)} custom-call(s32[9]{0:T(128)S(1)} %get-tuple-element.11.base_ref, bf16[256,32,128]{2,1,0:T(8,128)(2,1)} %collective-permute-done.2.refs_0_, bf16[256,32,128]{2,1,0:T(8,128)(2,1)} %collective-permute-done.5.refs_1_, ...), custom_call_target="tpu_custom_call", output_to_operand_aliasing={{}: (6, {})} | custom-call | flops 17179869184 | bytes 41943040 | tf_op jit(solution)/shard_map/pallas_call | solution.py:113
  (12 shorter events, 0.1 us)
Async XLA Ops:
  6.5 245.8 %all-gather.2.cloned.1.call-start = ((), (), s32[]{:S(2)}) async-start(), calls=%async_computation | async-start | bytes 37748736 | tf_op jit(solution)/shard_map/all_gather | solution.py:147
  27.0 3.4 copy-start
  27.0 3.4 copy-start.3
  63.9 95.5 %copy-start.2 = (bf16[256,32,128]{2,1,0:T(8,128)(2,1)}, bf16[256,32,128]{2,1,0:T(8,128)(2,1)S(1)}, u32[]{:S(2)}) copy-start(bf16[256,32,128]{2,1,0:T(8,128)(2,1)S(1)} %get-tuple-element.8.refs_0_) | copy-start | bytes 6291460
  63.9 188.4 %copy-start.1 = (bf16[256,32,128]{2,1,0:T(8,128)(2,1)}, bf16[256,32,128]{2,1,0:T(8,128)(2,1)S(1)}, u32[]{:S(2)}) copy-start(bf16[256,32,128]{2,1,0:T(8,128)(2,1)S(1)} %get-tuple-element.7.refs_1_) | copy-start | bytes 6291460
  63.9 51.7 %collective-permute-start = (bf16[256,32,128]{2,1,0:T(8,128)(2,1)S(1)}, bf16[256,32,128]{2,1,0:T(8,128)(2,1)}, u32[]{:S(2)}, u32[]{:S(2)}) collective-permute-start(bf16[256,32,128]{2,1,0:T(8,128)(2,1)S(1)} %get-tuple-element.8.refs_0_), channel_id=1, source_target_pairs={{0,1},{1,2},{2,3},{3,0},{4,5},{5,6},{6,7},{7,4},{8,9},{9,10},{10,1... | collective-permute-start | bytes 6291464 | tf_op jit(solution)/shard_map/ppermute | solution.py:171
  67.0 92.4 %collective-permute-start.3 = (bf16[256,32,128]{2,1,0:T(8,128)(2,1)S(1)}, bf16[256,32,128]{2,1,0:T(8,128)(2,1)}, u32[]{:S(2)}, u32[]{:S(2)}) collective-permute-start(bf16[256,32,128]{2,1,0:T(8,128)(2,1)S(1)} %get-tuple-element.7.refs_1_), channel_id=1, source_target_pairs={{0,3},{1,0},{2,1},{3,2},{4,7},{5,4},{6,5},{7,6},{8,11},{9,8},{10,9... | collective-permute-start | bytes 6291464 | tf_op jit(solution)/shard_map/ppermute | solution.py:172
  115.7 91.7 %collective-permute-start.1 = (bf16[256,32,128]{2,1,0:T(8,128)(2,1)}, bf16[256,32,128]{2,1,0:T(8,128)(2,1)}, u32[]{:S(2)}, u32[]{:S(2)}) collective-permute-start(bf16[256,32,128]{2,1,0:T(8,128)(2,1)} %collective-permute-done.refs_0_), channel_id=1, source_target_pairs={{0,1},{1,2},{2,3},{3,0},{4,5},{5,6},{6,7},{7,4},{8,9},{9,10},{10,1... | collective-permute-start | bytes 6291464 | tf_op jit(solution)/shard_map/ppermute | solution.py:171
  159.4 92.9 %collective-permute-start.4 = (bf16[256,32,128]{2,1,0:T(8,128)(2,1)}, bf16[256,32,128]{2,1,0:T(8,128)(2,1)}, u32[]{:S(2)}, u32[]{:S(2)}) collective-permute-start(bf16[256,32,128]{2,1,0:T(8,128)(2,1)} %collective-permute-done.3.refs_1_), channel_id=1, source_target_pairs={{0,3},{1,0},{2,1},{3,2},{4,7},{5,4},{6,5},{7,6},{8,11},{9,8},{10,9... | collective-permute-start | bytes 6291464 | tf_op jit(solution)/shard_map/ppermute | solution.py:172
  207.4 293.9 %collective-permute-start.2 = (bf16[256,32,128]{2,1,0:T(8,128)(2,1)}, bf16[256,32,128]{2,1,0:T(8,128)(2,1)}, u32[]{:S(2)}, u32[]{:S(2)}) collective-permute-start(bf16[256,32,128]{2,1,0:T(8,128)(2,1)} %collective-permute-done.1.refs_0_), channel_id=1, source_target_pairs={{0,1},{1,2},{2,3},{3,0},{4,5},{5,6},{6,7},{7,4},{8,9},{9,10},{10,1... | collective-permute-start | bytes 6291464 | tf_op jit(solution)/shard_map/ppermute | solution.py:171
  252.3 249.0 %collective-permute-start.5 = (bf16[256,32,128]{2,1,0:T(8,128)(2,1)}, bf16[256,32,128]{2,1,0:T(8,128)(2,1)}, u32[]{:S(2)}, u32[]{:S(2)}) collective-permute-start(bf16[256,32,128]{2,1,0:T(8,128)(2,1)} %collective-permute-done.4.refs_1_), channel_id=1, source_target_pairs={{0,3},{1,0},{2,1},{3,2},{4,7},{5,4},{6,5},{7,6},{8,11},{9,8},{10,9... | collective-permute-start | bytes 6291464 | tf_op jit(solution)/shard_map/ppermute | solution.py:172
Sparse Core Ops, SparseCore 0:
  59.4 163.4 all-gather.1
